TPU v7x, 32 devices: a whole 2x2x4 slice. The times are simulated.
32 devices in a mesh: dp: 8 (over z, x), rep: 4 (over y, core).
Axes of the slice: x: 2, y: 2, z: 4, core: 2. Of those that a mesh axis runs over, the one named last changes fastest.
Arguments:
- feats: bfloat16 [3072, 4, 4, 512], P(('dp', 'rep')), may hold values from -6 to 6
- labels: int32 [3072], P(('dp', 'rep')), may hold values from 0 to 9
- task_ids: int32 [3072], P(('dp', 'rep')), may hold values from 0 to 9, as said below
- live: int32 [3072], P(('dp', 'rep')), may hold values from 0 to 1, as said below
- branch: int32 [3072], P(('dp', 'rep')), may hold values from 0 to 1, as said below
- mem_counts: int32 [9], replicated, may hold values from 20 to 256
- conv_master: float32 [2, 4608, 512], P(None, None, 'rep'), may hold values from -0.09375 to 0.09375
- conv_rows: float32 [2, 4608], replicated, may hold values from 9.765625e-09 to 3.90625e-08
- conv_cols: float32 [2, 512], P(None, 'rep'), may hold values from 9.765625e-09 to 3.90625e-08
- head_master: float32 [512, 100], replicated, may hold values from -0.26516504 to 0.26516504
- head_rows: float32 [512], replicated, may hold values from 8.138021e-07 to 3.2552084e-06
- head_cols: float32 [100], replicated, may hold values from 8.138021e-06 to 3.2552085e-05
- head_bias: float32 [100], replicated, may hold values from -1.8 to 1.8
- head_bias_moment: float32 [100], replicated, may hold values from 2.2786458e-05 to 9.1145834e-05
- norm_gain: float32 [2, 512], replicated, may hold values from 0.25 to 2
- norm_bias: float32 [2, 512], replicated, may hold values from -1.8 to 1.8
- norm_moment: float32 [2, 2, 512], replicated, may hold values from 2.6041667e-08 to 1.04166666e-07
Outputs:
- cur_losses: float32 [2], replicated
- mem_losses: float32 [2], replicated
- agreement: float32 [2], replicated
- conv_grad: float32 [2, 4608, 512], P(None, None, 'rep')
- conv_rows_new: float32 [2, 4608], replicated
- conv_cols_new: float32 [2, 512], P(None, 'rep')
- conv_new: float32 [2, 4608, 512], P(None, None, 'rep')
- conv_copy_new: bfloat16 [2, 4608, 512], P(None, None, 'rep')
- head_grad: float32 [512, 100], replicated
- head_rows_new: float32 [512], replicated
- head_cols_new: float32 [100], replicated
- head_new: float32 [512, 100], replicated
- head_copy_new: bfloat16 [512, 100], replicated
- head_bias_grad: float32 [100], replicated
- head_bias_moment_new: float32 [100], replicated
- head_bias_new: float32 [100], replicated
- norm_grad: float32 [2, 2, 512], replicated
- norm_moment_new: float32 [2, 2, 512], replicated
- norm_new: float32 [2, 2, 512], replicated
Inputs may be any that keep to these rules, and one draw needn't show every extreme that they name: Each device's first two rows are live. `branch`: each device's first row is a current row and its second a memory row. `task_ids`: memory rows name past tasks 0 to 8; current rows name task 10 - 1.
All inputs are finite; a program needn't handle non-finite values.
Results may differ from a plain program's by a relative error of at most 0.015.
Values may be sent and summed in bfloat16 or wider, within the bound.
No kernel may reach another device: no remote copies, remote signals or barrier semaphores. Data moves between devices by JAX's collectives and lax.ppermute only.
A program may use at most 256 MiB of HBM per device.

v0:
```python
import jax
import jax.numpy as jnp
from jax import lax
from jax.sharding import PartitionSpec as P

CLASSES = 10
TASKS = 10
STEP = 10


norm_eps = 1e-05
eps_one = 1e-30
eps_two = 0.001
rel_step = 0.5
clip_level = 1.0


def convolve(feature_map, kernel):
    channels = feature_map.shape[3]
    map_side = feature_map.shape[1]
    padded = jnp.pad(feature_map, ((0, 0), (1, 1), (1, 1), (0, 0)))
    running = jnp.zeros(feature_map.shape[:3] + (kernel.shape[1],), jnp.float32)
    for tap_index in range(9):
        row_off = tap_index // 3
        col_off = tap_index % 3
        window = padded[:, row_off : row_off + map_side, col_off : col_off + map_side, :]
        running = running + jnp.einsum(
            "spqc,cd->spqd",
            window,
            kernel[tap_index * channels : (tap_index + 1) * channels],
            preferred_element_type=jnp.float32,
        )
    return running


def convolve_back(grad_map, kernel):
    channels = grad_map.shape[4]
    map_side = grad_map.shape[2]
    padded = jnp.pad(grad_map, ((0, 0), (0, 0), (1, 1), (1, 1), (0, 0)))
    running = jnp.zeros(grad_map.shape, jnp.float32)
    for tap_index in range(9):
        row_off = 2 - tap_index // 3
        col_off = 2 - tap_index % 3
        window = padded[:, :, row_off : row_off + map_side, col_off : col_off + map_side, :]
        running = running + jnp.einsum(
            "tspqd,cd->tspqc",
            window,
            kernel[tap_index * channels : (tap_index + 1) * channels],
            preferred_element_type=jnp.float32,
        )
    return running


def layer_grad(feature_map, grad_map):
    map_side = feature_map.shape[1]
    padded = jnp.pad(feature_map, ((0, 0), (1, 1), (1, 1), (0, 0)))
    pieces = []
    for tap_index in range(9):
        row_off = tap_index // 3
        col_off = tap_index % 3
        window = padded[:, row_off : row_off + map_side, col_off : col_off + map_side, :]
        pieces.append(
            jnp.einsum("spqc,tspqd->ctd", window, grad_map, preferred_element_type=jnp.float32)
        )
    return lax.psum_scatter(
        jnp.concatenate(pieces, axis=0).astype(jnp.bfloat16), "rep", scatter_dimension=2, tiled=True
    ).astype(jnp.float32)


def silu_slope(inputs):
    sig_gate = jax.nn.sigmoid(inputs)
    return sig_gate * (1.0 + inputs * (1.0 - sig_gate))


def moments(hidden, live_rows):
    masked = hidden * live_rows[:, None, None, None]
    return (jnp.sum(masked, axis=(0, 1, 2)), jnp.sum(masked * hidden, axis=(0, 1, 2)))


def norm_apply(hidden, stat_sum, stat_square, norm_count, gain, bias):
    mean_val = stat_sum / norm_count
    norm_scale = lax.rsqrt(stat_square / norm_count - mean_val * mean_val + norm_eps)
    normed = (hidden - mean_val) * norm_scale
    return (normed, norm_scale, normed * gain + bias)


def norm_back(upstream, normed, norm_scale, gain, live_rows, norm_count):
    local_bias = jnp.sum(upstream, axis=(1, 2, 3))
    local_gain = jnp.sum(upstream * normed, axis=(1, 2, 3))
    bias_grad, gain_grad = lax.psum((local_bias, local_gain), ("dp", "rep"))
    centered = (
        upstream
        - (bias_grad[:, None, None, None, :] + normed * gain_grad[:, None, None, None, :])
        / norm_count
    )
    hidden_grad = centered * (gain * norm_scale) * live_rows[None, :, None, None, None]
    return (hidden_grad.astype(jnp.bfloat16), gain_grad, bias_grad)


def factored(weight, grad_mat, row_stat, col_stat, decay_rate):
    square = grad_mat * grad_mat + eps_one
    new_rows = decay_rate * row_stat + (1.0 - decay_rate) * jnp.mean(square, axis=-1)
    new_cols = decay_rate * col_stat + (1.0 - decay_rate) * jnp.mean(square, axis=-2)
    second_est = (
        new_rows[..., :, None]
        * new_cols[..., None, :]
        / jnp.mean(new_rows, axis=-1)[..., None, None]
    )
    update = grad_mat * lax.rsqrt(second_est)
    update = update / jnp.maximum(
        1.0, jnp.sqrt(jnp.mean(update * update, axis=(-2, -1), keepdims=True)) / clip_level
    )
    step_size = rel_step * jnp.maximum(
        eps_two, jnp.sqrt(jnp.mean(weight * weight, axis=(-2, -1), keepdims=True))
    )
    return (new_rows, new_cols, weight - step_size * update)


def plain(weight, grad_vec, moment, decay_rate):
    new_moment = decay_rate * moment + (1.0 - decay_rate) * (grad_vec * grad_vec + eps_one)
    update = grad_vec * lax.rsqrt(new_moment)
    update = update / jnp.maximum(
        1.0, jnp.sqrt(jnp.mean(update * update, axis=-1, keepdims=True)) / clip_level
    )
    step_size = rel_step * jnp.maximum(
        eps_two, jnp.sqrt(jnp.mean(weight * weight, axis=-1, keepdims=True))
    )
    return (new_moment, weight - step_size * update)


def local(
    feats,
    labels,
    task_ids,
    live,
    branch,
    mem_counts,
    conv_master,
    conv_rows,
    conv_cols,
    head_master,
    head_rows,
    head_cols,
    head_bias,
    head_bias_moment,
    norm_gain,
    norm_bias,
    norm_moment,
):
    channels = feats.shape[3]
    map_side = feats.shape[1]
    decay_rate = 1.0 - STEP ** (-0.8)
    live_rows = live.astype(jnp.float32)
    memory = branch.astype(jnp.float32)
    past_tasks = jnp.arange(TASKS - 1)
    inverse = jnp.sum(
        jnp.where(
            task_ids[:, None] == past_tasks[None, :],
            1.0 / mem_counts.astype(jnp.float32)[None, :],
            0.0,
        ),
        axis=1,
    )
    cur_weight = live_rows * (1.0 - memory)
    mem_weight = live_rows * memory * inverse
    weights = jnp.stack([cur_weight, mem_weight])
    local_counts = jnp.stack([jnp.sum(live_rows), jnp.sum(cur_weight), jnp.sum(mem_weight)])
    kernels = lax.all_gather(conv_master.astype(jnp.bfloat16), "rep", axis=2, tiled=True)
    head_lowered = head_master.astype(jnp.bfloat16)
    first_map = convolve(feats, kernels[0])
    stat_sum, stat_square = moments(first_map, live_rows)
    totals = lax.psum(local_counts, ("dp", "rep"))
    stat_sum, stat_square = lax.psum((stat_sum, stat_square), ("dp", "rep"))
    norm_count = map_side * map_side * totals[0]
    normed_one, scale_one, pre_one = norm_apply(
        first_map, stat_sum, stat_square, norm_count, norm_gain[0], norm_bias[0]
    )
    activated = jax.nn.silu(pre_one).astype(jnp.bfloat16)
    second_map = convolve(activated, kernels[1])
    two_sum, two_square = moments(second_map, live_rows)
    two_sum, two_square = lax.psum((two_sum, two_square), ("dp", "rep"))
    normed_two, scale_two, pre_two = norm_apply(
        second_map, two_sum, two_square, norm_count, norm_gain[1], norm_bias[1]
    )
    joined = feats.astype(jnp.float32) + pre_two
    block_out = jax.nn.silu(joined)
    pooled = (jnp.sum(block_out, axis=(1, 2)) / (map_side * map_side)).astype(jnp.bfloat16)
    logits = jnp.dot(pooled, head_lowered, preferred_element_type=jnp.float32) + head_bias
    task_hot = (task_ids[:, None] == jnp.arange(TASKS)[None, :]).astype(jnp.float32)
    label_hot = (labels[:, None] == jnp.arange(CLASSES)[None, :]).astype(jnp.float32)
    chosen = jnp.sum(logits.reshape(-1, TASKS, CLASSES) * task_hot[:, :, None], axis=1)
    row_top = jnp.max(chosen, axis=1, keepdims=True)
    exp_terms = jnp.exp(chosen - row_top)
    exp_total = jnp.sum(exp_terms, axis=1, keepdims=True)
    entropy = row_top[:, 0] + jnp.log(exp_total[:, 0]) - jnp.sum(chosen * label_hot, axis=1)
    loss_terms = jnp.sum(weights * entropy[None, :], axis=1)
    scales = weights * (1.0 / jnp.stack([totals[1], totals[2]]))[:, None]
    dchosen = (exp_terms / exp_total - label_hot)[None] * scales[:, :, None]
    dlogits = (
        (dchosen[:, :, None, :] * task_hot[None, :, :, None])
        .reshape(2, -1, TASKS * CLASSES)
        .astype(jnp.bfloat16)
    )
    dpooled = jnp.einsum("tsk,ck->tsc", dlogits, head_lowered, preferred_element_type=jnp.float32)
    head_part = jnp.einsum("sc,tsk->tck", pooled, dlogits, preferred_element_type=jnp.float32)
    bias_part = jnp.sum(dlogits.astype(jnp.float32), axis=1)
    upstream = (dpooled / (map_side * map_side))[:, :, None, None, :] * silu_slope(joined)[None]
    hidden_two, gain_two, shift_two = norm_back(
        upstream, normed_two, scale_two, norm_gain[1], live_rows, norm_count
    )
    conv_two = layer_grad(activated, hidden_two)
    act_grad = convolve_back(hidden_two, kernels[1]) * silu_slope(pre_one)[None]
    hidden_one, gain_one, shift_one = norm_back(
        act_grad, normed_one, scale_one, norm_gain[0], live_rows, norm_count
    )
    conv_one = layer_grad(feats, hidden_one)
    stacked = jnp.stack([conv_one, conv_two])
    head_sum, bias_sum, loss_sum = lax.psum((head_part, bias_part, loss_terms), ("dp", "rep"))
    norm_both = jnp.stack(
        [jnp.stack([gain_one, gain_two], axis=1), jnp.stack([shift_one, shift_two], axis=1)], axis=1
    )
    small_dot = (
        jnp.sum(head_sum[0] * head_sum[1])
        + jnp.sum(bias_sum[0] * bias_sum[1])
        + jnp.sum(norm_both[0] * norm_both[1])
    )
    small_square = (
        jnp.sum(head_sum[1] * head_sum[1])
        + jnp.sum(bias_sum[1] * bias_sum[1])
        + jnp.sum(norm_both[1] * norm_both[1])
    )
    small_pair = jnp.stack([small_dot, small_square])
    conv_sum = lax.psum(stacked, "dp")
    partial_value = jnp.stack(
        [
            jnp.sum(conv_sum[:, :, 0] * conv_sum[:, :, 1]),
            jnp.sum(conv_sum[:, :, 1] * conv_sum[:, :, 1]),
        ]
    )
    agreement = lax.psum(partial_value, "rep") + small_pair
    project_coef = jnp.minimum(agreement[0], 0.0) / agreement[1]
    conv_grad = conv_sum[:, :, 0] - project_coef * conv_sum[:, :, 1]
    conv_square = conv_grad * conv_grad + eps_one
    conv_cols_new = decay_rate * conv_cols + (1.0 - decay_rate) * jnp.mean(conv_square, axis=1)
    row_part = jnp.sum(conv_square, axis=2)
    over_cols = jnp.sum(conv_grad * conv_grad / conv_cols_new[:, None, :], axis=2)
    weight_part = jnp.sum(conv_master * conv_master, axis=(1, 2))
    row_total, over_total, weight_total = (
        lax.psum(row_part.astype(jnp.bfloat16), "rep").astype(jnp.float32),
        lax.psum(over_cols.astype(jnp.bfloat16), "rep").astype(jnp.float32),
        lax.psum(weight_part.astype(jnp.bfloat16), "rep").astype(jnp.float32),
    )
    conv_rows_new = decay_rate * conv_rows + (1.0 - decay_rate) * row_total / channels
    row_mean = jnp.mean(conv_rows_new, axis=1)
    entries = conv_grad.shape[1] * channels
    update_rms = jnp.sqrt(row_mean * jnp.sum(over_total / conv_rows_new, axis=1) / entries)
    update = conv_grad * lax.rsqrt(
        conv_rows_new[:, :, None] * conv_cols_new[:, None, :] / row_mean[:, None, None]
    )
    update = update / jnp.maximum(1.0, update_rms / clip_level)[:, None, None]
    step_size = rel_step * jnp.maximum(eps_two, jnp.sqrt(weight_total / entries))
    conv_new = conv_master - step_size[:, None, None] * update
    head_grad = head_sum[0] - project_coef * head_sum[1]
    bias_grad = bias_sum[0] - project_coef * bias_sum[1]
    norm_grad = norm_both[0] - project_coef * norm_both[1]
    head_rows_new, head_cols_new, head_new = factored(
        head_master, head_grad, head_rows, head_cols, decay_rate
    )
    bias_moment_new, bias_new = plain(head_bias, bias_grad, head_bias_moment, decay_rate)
    norm_moment_new, norm_new = plain(
        jnp.stack([norm_gain, norm_bias]), norm_grad, norm_moment, decay_rate
    )
    cur_losses = jnp.stack([loss_sum[0], totals[1]])
    mem_losses = jnp.stack([loss_sum[1], totals[2]])
    return (
        cur_losses,
        mem_losses,
        agreement,
        conv_grad,
        conv_rows_new,
        conv_cols_new,
        conv_new,
        conv_new.astype(jnp.bfloat16),
        head_grad,
        head_rows_new,
        head_cols_new,
        head_new,
        head_new.astype(jnp.bfloat16),
        bias_grad,
        bias_moment_new,
        bias_new,
        norm_grad,
        norm_moment_new,
        norm_new,
    )


def solution(mesh):
    return jax.shard_map(
        local,
        mesh=mesh,
        in_specs=(
            P(("dp", "rep"), None, None, None),
            P(("dp", "rep")),
            P(("dp", "rep")),
            P(("dp", "rep")),
            P(("dp", "rep")),
            P(),
            P(None, None, "rep"),
            P(),
            P(None, "rep"),
            P(),
            P(),
            P(),
            P(),
            P(),
            P(),
            P(),
            P(),
        ),
        out_specs=(
            P(),
            P(),
            P(),
            P(None, None, "rep"),
            P(),
            P(None, "rep"),
            P(None, None, "rep"),
            P(None, None, "rep"),
            P(),
            P(),
            P(),
            P(),
            P(),
            P(),
            P(),
            P(),
            P(),
            P(),
            P(),
        ),
        check_vma=False,
    )
```

profile of v0, /device:TPU:0, one launch (start us, length us, event | category | flops | bytes accessed | tf_op | source)
XLA Modules:
  0.0 1099.2 jit_solution(12336366606190110409)
XLA Ops:
  7.3 6.7 multiply_reduce_fusion.2
  17.0 65.3 %all-gather.2.cloned.1.call-done = bf16[2,4608,512]{2,1,0:T(8,128)(2,1)} async-done(((bf16[2,4608,128]{2,1,0:T(8,128)(2,1)}), bf16[2,4608,512]{2,1,0:T(8,128)(2,1)}) %all-gather.2.cloned.1.call-update) | async-done | bytes 9437200 | tf_op jit(solution)/shard_map/all_gather | solution.py:168
  105.4 5.7 multiply_reduce_fusion.6
  111.1 39.6 %all-reduce.6 = (f32[3]{0:T(128)S(1)}, f32[512]{0:T(512)S(1)}, f32[512]{0:T(512)S(1)}) all-reduce(f32[3]{0:T(128)S(1)} %pad_maximum_fusion.3, f32[512]{0:T(512)S(1)} %get-tuple-element.30, f32[512]{0:T(512)S(1)} %get-tuple-element.29), channel_id=1, replica_groups=mesh['dp'=8,'rep'=4] {'dp','rep'}, use_global_device_ids=true, to_apply=%region_6.7 | all-reduce | flops 1027 | bytes 8216 | tf_op jit(solution)/shard_map/psum | solution.py:172
  178.4 5.1 multiply_reduce_fusion.5
  183.5 41.0 %all-reduce.5 = (f32[512]{0:T(512)S(1)}, f32[512]{0:T(512)S(1)}) all-reduce(f32[512]{0:T(512)S(1)} %get-tuple-element.28, f32[512]{0:T(512)S(1)} %get-tuple-element.27), channel_id=1, replica_groups=mesh['dp'=8,'rep'=4] {'dp','rep'}, use_global_device_ids=true, to_apply=%region_12.13 | all-reduce | flops 1024 | bytes 8192 | tf_op jit(solution)/shard_map/psum | solution.py:181
  225.1 5.2 add_multiply_fusion.2
  238.4 48.8 %all-reduce.4 = (f32[2,512]{1,0:T(2,128)S(1)}, f32[2,512]{1,0:T(2,128)S(1)}) all-reduce(f32[2,512]{1,0:T(2,128)S(1)} %get-tuple-element.26, f32[2,512]{1,0:T(2,128)S(1)} %get-tuple-element.25), channel_id=1, replica_groups=mesh['dp'=8,'rep'=4] {'dp','rep'}, use_global_device_ids=true, to_apply=%region_23.24 | all-reduce | flops 2048 | bytes 16384 | tf_op jit(solution)/shard_map/psum | solution.py:90
  316.2 24.0 %copy.197 = bf16[4608,2,512]{0,1,2:T(2,128)(2,1)} copy(bf16[4608,2,512]{2,0,1:T(8,128)(2,1)} %fusion.89) | data formatting | bytes 18874368
  340.3 9.6 copy.201
  354.2 6.3 fusion.107
  360.5 6.2 fusion.109
  366.8 5.6 fusion.111
  372.4 5.6 fusion.113
  378.0 5.5 fusion.115
  383.5 5.4 fusion.117
  388.9 5.5 fusion.121
  394.4 5.8 fusion.119
  400.2 21.6 %fusion.204 = (f32[2,512]{1,0:T(2,128)S(1)}, f32[2,512]{1,0:T(2,128)S(1)}, f32[2,96,4,4,512]{4,1,3,2,0:T(8,128)}) fusion(f32[96,4,4,512]{3,0,2,1:T(8,128)S(1)} %copy-done.5, f32[96,4,4,512]{3,0,2,1:T(8,128)} %get-tuple-element.80, bf16[2,96,4,4,512]{4,1,3,2,0:T(8,128)(2,1)S(1)} %fusion.3, bf16[2,4608,512]{2,1,0:T(8,128)(2,1)} %all-gather.2.cloned.1.call-done, ...), kind=kOutput, calls=%fused_computation.304 | convolution fusion | flops 924841984 | bytes 66592768 | tf_op jit(solution)/shard_map/tspqd,cd->tspqc/dot_general | solution.py:45
  421.8 41.4 %all-reduce.3 = (f32[2]{0:T(128)S(1)}, f32[2,512]{1,0:T(2,128)S(1)}, f32[2,512]{1,0:T(2,128)S(1)}, f32[2,100]{1,0:T(2,128)S(1)}) all-reduce(f32[2]{0:T(128)S(1)} %copy-done.42, f32[2,512]{1,0:T(2,128)S(1)} %get-tuple-element.22, f32[2,512]{1,0:T(2,128)S(1)} %get-tuple-element.21, ...), channel_id=1, replica_groups=mesh['dp'=8,'rep'=4] {'dp','rep'}, use_global_device_ids=true, to_apply=%region_19.20 | all-reduce | flops 2250 | bytes 18000 | tf_op jit(solution)/shard_map/psum | solution.py:218
  493.8 24.2 %copy.195 = bf16[4608,2,512]{0,1,2:T(2,128)(2,1)} copy(bf16[4608,2,512]{2,0,1:T(8,128)(2,1)} %fusion.62) | data formatting | bytes 18874368
  518.0 9.7 copy.200
  534.6 6.2 copy.198
  540.7 65.4 %reduce-scatter.7.cloned.1.call-done = bf16[128,9216]{1,0:T(8,128)(2,1)} async-done(((bf16[512,9216]{1,0:T(8,128)(2,1)}), bf16[128,9216]{1,0:T(8,128)(2,1)}) %reduce-scatter.7.cloned.1.call-update) | async-done | bytes 2359312
  610.8 6.8 copy.196
  617.6 5.9 maximum_convert_fusion
  632.3 105.5 %all-reduce.13.cloned.1.call-done = f32[2,512,100]{1,2,0:T(8,128)} async-done(((f32[2,512,100]{1,2,0:T(8,128)}), f32[2,512,100]{1,2,0:T(8,128)}) %all-reduce.13.cloned.1.call-update) | async-done | bytes 409616 | tf_op jit(solution)/shard_map/psum | solution.py:218
  742.7 298.4 %all-reduce.11.cloned.1.call-done = f32[2,4608,2,128]{3,1,2,0:T(8,128)} async-done(((f32[2,4608,2,128]{3,1,2,0:T(8,128)}), f32[2,4608,2,128]{3,1,2,0:T(8,128)}) %all-reduce.11.cloned.1.call-update) | async-done | bytes 9437200 | tf_op jit(solution)/shard_map/psum | solution.py:233
  1041.1 5.6 multiply_reduce_fusion.4
  1048.7 6.8 psum.130
  1066.9 10.7 all-reduce.7
  1083.0 8.0 fusion.209
  (231 shorter events, 161.8 us)
Async XLA Ops:
  7.2 6.9 copy-start.50
  7.2 7.1 copy-start.54
  7.2 7.2 copy-start.52
  7.2 9.8 copy-start.23
  7.2 9.8 copy-start.25
  7.3 75.1 %copy-start.2 = (bf16[96,4,4,512]{3,2,1,0:T(4,128)(2,1)S(1)}, bf16[96,4,4,512]{3,2,1,0:T(4,128)(2,1)}, u32[]{:S(2)}) copy-start(bf16[96,4,4,512]{3,2,1,0:T(4,128)(2,1)} %param.17) | copy-start | bytes 4718596
  7.3 75.1 %all-gather.2.cloned.1.call-start = ((), (), s32[]{:S(2)}) async-start(), calls=%async_computation.2 | async-start | bytes 11796480 | tf_op jit(solution)/shard_map/all_gather | solution.py:168
  14.0 515.7 %reduce-scatter.9.cloned.1.call-start = ((), (), s32[]{:S(2)}) async-start(), calls=%async_computation.6 | async-start | bytes 11796480
  14.1 164.3 %copy-start.35 = (f32[96]{0:T(128)}, f32[96]{0:T(128)S(1)}, u32[]{:S(2)}) copy-start(f32[96]{0:T(128)S(1)} %convert_element_type.93) | copy-start | bytes 1156
  14.3 220.1 %copy-start.17 = (f32[96,100]{1,0:T(8,128)}, f32[96,100]{1,0:T(8,128)S(1)}, u32[]{:S(2)}) copy-start(f32[96,100]{1,0:T(8,128)S(1)} %copy.107) | copy-start | bytes 115204
  158.5 19.9 %copy-start = (bf16[96,4,4,512]{3,0,2,1:T(8,128)(2,1)}, bf16[96,4,4,512]{3,0,2,1:T(8,128)(2,1)S(1)}, u32[]{:S(2)}) copy-start(bf16[96,4,4,512]{3,0,2,1:T(8,128)(2,1)S(1)} %multiply_convert_fusion.1) | copy-start | bytes 4718596
  349.9 256.2 %reduce-scatter.7.cloned.1.call-start = ((), (), s32[]{:S(2)}) async-start(), calls=%async_computation.5 | async-start | bytes 11796480
  400.2 21.6 %copy-start.42 = (f32[2]{0:T(128)S(1)}, f32[2]{0:T(128)}, u32[]{:S(2)}) copy-start(f32[2]{0:T(128)} %get-tuple-element.96) | copy-start | bytes 28
  400.2 63.0 %copy-start.36 = (f32[96]{0:T(128)S(1)}, f32[96]{0:T(128)}, u32[]{:S(2)}) copy-start(f32[96]{0:T(128)} %copy-done.35) | copy-start | bytes 1156
  400.2 63.0 %copy-start.37 = (f32[512]{0:T(512)S(1)}, f32[512]{0:T(512)}, u32[]{:S(2)}) copy-start(f32[512]{0:T(512)} %get-tuple-element.78) | copy-start | bytes 6148
  527.7 210.0 %all-reduce.13.cloned.1.call-start = ((), (), s32[]{:S(2)}) async-start(), calls=%async_computation.4 | async-start | bytes 851968 | tf_op jit(solution)/shard_map/psum | solution.py:218
  529.7 511.4 %all-reduce.11.cloned.1.call-start = ((), (), s32[]{:S(2)}) async-start(), calls=%async_computation.3 | async-start | bytes 18874368 | tf_op jit(solution)/shard_map/psum | solution.py:233
  1062.1 15.5 %copy-start.13 = (f32[2,512,100]{1,2,0:T(8,128)S(1)}, f32[2,512,100]{1,2,0:T(8,128)}, u32[]{:S(2)}) copy-start(f32[2,512,100]{1,2,0:T(8,128)} %all-reduce.13.cloned.1.call-done) | copy-start | bytes 1228804
  1062.2 15.6 %copy-start.43 = (f32[512]{0:T(512)S(1)}, f32[512]{0:T(512)}, u32[]{:S(2)}) copy-start(f32[512]{0:T(512)} %param.27) | copy-start | bytes 6148
  1062.2 16.2 %copy-start.55 = (f32[100]{0:T(128)S(1)}, f32[100]{0:T(128)}, u32[]{:S(2)}) copy-start(f32[100]{0:T(128)} %param.28) | copy-start | bytes 1204
  1062.2 18.3 %copy-start.51 = (f32[100]{0:T(128)S(1)}, f32[100]{0:T(128)}, u32[]{:S(2)}) copy-start(f32[100]{0:T(128)} %param.30) | copy-start | bytes 1204
  1062.2 19.6 %copy-start.38 = (f32[2,2,512]{2,1,0:T(2,128)S(1)}, f32[2,2,512]{2,1,0:T(2,128)}, u32[]{:S(2)}) copy-start(f32[2,2,512]{2,1,0:T(2,128)} %param.33) | copy-start | bytes 24580
  1062.2 19.8 %copy-start.22 = (f32[2,4608]{1,0:T(2,128)S(1)}, f32[2,4608]{1,0:T(2,128)}, u32[]{:S(2)}) copy-start(f32[2,4608]{1,0:T(2,128)} %param.24) | copy-start | bytes 110596
  1062.2 20.8 %copy-start.34 = (f32[2,128]{1,0:T(2,128)}, f32[2,128]{1,0:T(2,128)S(1)}, u32[]{:S(2)}) copy-start(f32[2,128]{1,0:T(2,128)S(1)} %multiply_add_fusion.5) | copy-start | bytes 3076
  1077.8 13.3 %copy-start.10 = (f32[512,100]{0,1:T(8,128)}, f32[512,100]{0,1:T(8,128)S(1)}, u32[]{:S(2)}) copy-start(f32[512,100]{0,1:T(8,128)S(1)} %get-tuple-element.70) | copy-start | bytes 614404
  1078.4 12.7 %copy-start.29 = (f32[512]{0:T(512)}, f32[512]{0:T(512)S(1)}, u32[]{:S(2)}) copy-start(f32[512]{0:T(512)S(1)} %get-tuple-element.69) | copy-start | bytes 6148
  1078.4 12.7 %copy-start.46 = (f32[100]{0:T(128)}, f32[100]{0:T(128)S(1)}, u32[]{:S(2)}) copy-start(f32[100]{0:T(128)S(1)} %multiply_add_fusion.7) | copy-start | bytes 1204
  1081.1 10.0 copy-start.44
  1081.1 10.0 copy-start.45
  1081.9 9.7 copy-start.27
  1081.9 9.7 copy-start.28
  1082.2 8.9 copy-start.19
  (29 other events, 92.2 us)
Sparse Core Ops, SparseCore 0:
  14.2 68.1 all-gather.1
  350.0 79.1 reduce-scatter.8
  527.8 78.2 reduce-scatter.6
  611.9 125.8 all-reduce.12
  741.9 299.1 all-reduce.10
where the time goes:
time: 1110 us; the launch traced here: 1100 us
  waiting for transfers between devices  535 us (48%)
  blocking collectives  188 us (17%)
  matrix products  174 us (16%)
  local copies, waits for them, and re-layouts  101 us (9%)
  other arithmetic  76.4 us (7%)
  between operations  24.3 us (2%)
    psum x1, waiting for transfers between devices, local(): conv_sum = lax.psum(stacked, 'dp')  298 us
    psum x1, waiting for transfers between devices, local(): lax.psum((head_part, bias_part, loss_terms), ('dp', 'rep'))  105 us
    unnamed x121, local copies, waits for them, and re-layouts  98.9 us
    dot_general x9, matrix products, convolve_back(): jnp.einsum('tspqd,cd->tspqc', window, kernel[tap_index * channels:(tap_in...  67.5 us
    unnamed x7, waiting for transfers between devices  65.5 us
    all_gather x1, waiting for transfers between devices, local(): lax.all_gather(conv_master.astype(jnp.bfloat16), 'rep', axis=2, tiled=True)  65.3 us
    dot_general x18, matrix products, convolve(): jnp.einsum('spqc,cd->spqd', window, kernel[tap_index * channels:(tap_inde...  53.7 us
    dot_general x18, matrix products, layer_grad(): jnp.einsum('spqc,tspqd->ctd', window, grad_map, preferred_element_type=jn...  51.1 us
  transfers between devices with their start and end apart: 5, of which 4 were waited for; matrix products, arithmetic and copies ran while one was open for 16% of the time, Pallas kernels for 0%

commit v1 on v0

--- a/solution.py
+++ b/solution.py
@@ -15,17 +15,103 @@
 clip_level = 1.0
 
 
+def swap(x, axis, bit):
+    n = lax.axis_size(axis)
+    return lax.ppermute(x, axis, [(i, i ^ bit) for i in range(n)])
+
+
+def bits_of(n):
+    return [1 << k for k in range(n.bit_length() - 1)]
+
+
+def exchange_sum(x, axis, basis):
+    first = x + swap(x, axis, basis[0]) if len(basis) == 1 else None
+    if first is not None:
+        return first
+    a, b = basis
+    return (x + swap(x, axis, a)) + (swap(x, axis, b) + swap(x, axis, a ^ b))
+
+
+def axis_sum(x, axis):
+    bits = bits_of(lax.axis_size(axis))
+    if len(bits) % 2:
+        x = exchange_sum(x, axis, bits[:1])
+        bits = bits[1:]
+    while bits:
+        x = exchange_sum(x, axis, bits[:2])
+        bits = bits[2:]
+    return x
+
+
+def all_sum(x):
+    return axis_sum(axis_sum(x, "rep"), "dp")
+
+
+def coord(axis, bit):
+    return (lax.axis_index(axis) & bit) // bit
+
+
+def pick(x, dim, index):
+    return lax.dynamic_index_in_dim(x, index, dim, keepdims=False)
+
+
+def halve(x, dim, axis, bit):
+    mine = coord(axis, bit)
+    other = swap(pick(x, dim, 1 - mine), axis, bit)
+    return (pick(x, dim, mine).astype(jnp.float32) + other.astype(jnp.float32)).astype(x.dtype)
+
+
+def double(x, dim, axis, bit):
+    other = swap(x, axis, bit)
+    mine = coord(axis, bit) == 0
+    return jnp.stack([jnp.where(mine, x, other), jnp.where(mine, other, x)], axis=dim)
+
+
+def orders(nrep, ndp):
+    rep_bits = [("rep", b) for b in bits_of(nrep)]
+    dp_bits = [("dp", b) for b in bits_of(ndp)]
+    core, rest = rep_bits[:1], rep_bits[1:]
+    return [
+        core + rest + dp_bits,
+        core + dp_bits[:1] + rest + dp_bits[1:],
+        core + dp_bits[1:] + dp_bits[:1] + rest,
+    ]
+
+
+def labels_of(nrep, ndp):
+    return [("rep", b) for b in reversed(bits_of(nrep))] + [("dp", b) for b in reversed(bits_of(ndp))]
+
+
+def scatter(x, order, nrep, ndp):
+    names = labels_of(nrep, ndp)
+    for key in order:
+        dim = names.index(key)
+        x = halve(x, dim, *key)
+        names.pop(dim)
+    return x
+
+
+def gather_dp(x, order, ndp):
+    target = [("dp", b) for b in reversed(bits_of(ndp))]
+    names = []
+    for key in reversed([k for k in order if k[0] == "dp"]):
+        dim = sum(target.index(n) < target.index(key) for n in names)
+        x = double(x, dim, *key)
+        names.insert(dim, key)
+    return x
+
+
 def convolve(feature_map, kernel):
     channels = feature_map.shape[3]
-    map_side = feature_map.shape[1]
-    padded = jnp.pad(feature_map, ((0, 0), (1, 1), (1, 1), (0, 0)))
-    running = jnp.zeros(feature_map.shape[:3] + (kernel.shape[1],), jnp.float32)
+    map_side = feature_map.shape[0]
+    padded = jnp.pad(feature_map, ((1, 1), (1, 1), (0, 0), (0, 0)))
+    running = 0.0
     for tap_index in range(9):
         row_off = tap_index // 3
         col_off = tap_index % 3
-        window = padded[:, row_off : row_off + map_side, col_off : col_off + map_side, :]
+        window = padded[row_off : row_off + map_side, col_off : col_off + map_side]
         running = running + jnp.einsum(
-            "spqc,cd->spqd",
+            "pqsc,cd->pqsd",
             window,
             kernel[tap_index * channels : (tap_index + 1) * channels],
             preferred_element_type=jnp.float32,
@@ -35,15 +121,15 @@
 
 def convolve_back(grad_map, kernel):
     channels = grad_map.shape[4]
-    map_side = grad_map.shape[2]
-    padded = jnp.pad(grad_map, ((0, 0), (0, 0), (1, 1), (1, 1), (0, 0)))
-    running = jnp.zeros(grad_map.shape, jnp.float32)
+    map_side = grad_map.shape[1]
+    padded = jnp.pad(grad_map, ((0, 0), (1, 1), (1, 1), (0, 0), (0, 0)))
+    running = 0.0
     for tap_index in range(9):
         row_off = 2 - tap_index // 3
         col_off = 2 - tap_index % 3
-        window = padded[:, :, row_off : row_off + map_side, col_off : col_off + map_side, :]
+        window = padded[:, row_off : row_off + map_side, col_off : col_off + map_side]
         running = running + jnp.einsum(
-            "tspqd,cd->tspqc",
+            "tpqsd,cd->tpqsc",
             window,
             kernel[tap_index * channels : (tap_index + 1) * channels],
             preferred_element_type=jnp.float32,
@@ -51,20 +137,26 @@
     return running
 
 
-def layer_grad(feature_map, grad_map):
-    map_side = feature_map.shape[1]
-    padded = jnp.pad(feature_map, ((0, 0), (1, 1), (1, 1), (0, 0)))
-    pieces = []
-    for tap_index in range(9):
-        row_off = tap_index // 3
-        col_off = tap_index % 3
-        window = padded[:, row_off : row_off + map_side, col_off : col_off + map_side, :]
-        pieces.append(
-            jnp.einsum("spqc,tspqd->ctd", window, grad_map, preferred_element_type=jnp.float32)
-        )
-    return lax.psum_scatter(
-        jnp.concatenate(pieces, axis=0).astype(jnp.bfloat16), "rep", scatter_dimension=2, tiled=True
-    ).astype(jnp.float32)
+def layer_grad(feature_map, grad_map, nrep, ndp):
+    map_side = feature_map.shape[0]
+    channels = feature_map.shape[3]
+    padded = jnp.pad(feature_map, ((1, 1), (1, 1), (0, 0), (0, 0)))
+    shards = []
+    for part, order in enumerate(orders(nrep, ndp)):
+        pieces = []
+        for tap_index in range(3 * part, 3 * part + 3):
+            row_off = tap_index // 3
+            col_off = tap_index % 3
+            window = padded[row_off : row_off + map_side, col_off : col_off + map_side]
+            pieces.append(
+                jnp.einsum("pqsc,tpqsd->tcd", window, grad_map, preferred_element_type=jnp.float32)
+            )
+        block = jnp.stack(pieces).astype(jnp.bfloat16)
+        block = block.reshape(3, 2, ndp, channels // ndp, nrep, channels // nrep)
+        block = block.transpose(4, 2, 0, 1, 3, 5)
+        lead = [2] * (len(bits_of(nrep)) + len(bits_of(ndp)))
+        shards.append(scatter(block.reshape(*lead, *block.shape[2:]), order, nrep, ndp))
+    return shards
 
 
 def silu_slope(inputs):
@@ -73,8 +165,8 @@
 
 
 def moments(hidden, live_rows):
-    masked = hidden * live_rows[:, None, None, None]
-    return (jnp.sum(masked, axis=(0, 1, 2)), jnp.sum(masked * hidden, axis=(0, 1, 2)))
+    masked = hidden * live_rows[None, None, :, None]
+    return jnp.stack([jnp.sum(masked, axis=(0, 1, 2)), jnp.sum(masked * hidden, axis=(0, 1, 2))])
 
 
 def norm_apply(hidden, stat_sum, stat_square, norm_count, gain, bias):
@@ -87,13 +179,13 @@
 def norm_back(upstream, normed, norm_scale, gain, live_rows, norm_count):
     local_bias = jnp.sum(upstream, axis=(1, 2, 3))
     local_gain = jnp.sum(upstream * normed, axis=(1, 2, 3))
-    bias_grad, gain_grad = lax.psum((local_bias, local_gain), ("dp", "rep"))
+    bias_grad, gain_grad = all_sum(jnp.stack([local_bias, local_gain]))
     centered = (
         upstream
         - (bias_grad[:, None, None, None, :] + normed * gain_grad[:, None, None, None, :])
         / norm_count
     )
-    hidden_grad = centered * (gain * norm_scale) * live_rows[None, :, None, None, None]
+    hidden_grad = centered * (gain * norm_scale) * live_rows[None, None, None, :, None]
     return (hidden_grad.astype(jnp.bfloat16), gain_grad, bias_grad)
 
 
@@ -128,7 +220,19 @@
     return (new_moment, weight - step_size * update)
 
 
+def gather_kernels(lowered, nrep):
+    held = lowered[None]
+    for bit in reversed(bits_of(nrep)):
+        other = swap(held, "rep", bit)
+        low = coord("rep", bit) == 0
+        held = jnp.stack([jnp.where(low, held, other), jnp.where(low, other, held)], axis=1)
+        held = held.reshape((-1,) + lowered.shape)
+    return held.transpose(1, 0, 2).reshape(lowered.shape[0], -1)
+
+
 def local(
+    nrep,
+    ndp,
     feats,
     labels,
     task_ids,
@@ -149,6 +253,7 @@
 ):
     channels = feats.shape[3]
     map_side = feats.shape[1]
+    area = map_side * map_side
     decay_rate = 1.0 - STEP ** (-0.8)
     live_rows = live.astype(jnp.float32)
     memory = branch.astype(jnp.float32)
@@ -165,26 +270,30 @@
     mem_weight = live_rows * memory * inverse
     weights = jnp.stack([cur_weight, mem_weight])
     local_counts = jnp.stack([jnp.sum(live_rows), jnp.sum(cur_weight), jnp.sum(mem_weight)])
-    kernels = lax.all_gather(conv_master.astype(jnp.bfloat16), "rep", axis=2, tiled=True)
+    kernel_one = gather_kernels(conv_master[0].astype(jnp.bfloat16), nrep)
+    kernel_two = gather_kernels(conv_master[1].astype(jnp.bfloat16), nrep)
     head_lowered = head_master.astype(jnp.bfloat16)
-    first_map = convolve(feats, kernels[0])
-    stat_sum, stat_square = moments(first_map, live_rows)
-    totals = lax.psum(local_counts, ("dp", "rep"))
-    stat_sum, stat_square = lax.psum((stat_sum, stat_square), ("dp", "rep"))
-    norm_count = map_side * map_side * totals[0]
+    feats_pos = feats.transpose(1, 2, 0, 3)
+    first_map = convolve(feats_pos, kernel_one)
+    stats = moments(first_map, live_rows)
+    packed = jnp.concatenate([stats.reshape(-1), local_counts])
+    packed = all_sum(jnp.pad(packed, (0, -packed.shape[0] % 128)))
+    stat_sum = packed[:channels]
+    stat_square = packed[channels : 2 * channels]
+    totals = packed[2 * channels : 2 * channels + 3]
+    norm_count = area * totals[0]
     normed_one, scale_one, pre_one = norm_apply(
         first_map, stat_sum, stat_square, norm_count, norm_gain[0], norm_bias[0]
     )
     activated = jax.nn.silu(pre_one).astype(jnp.bfloat16)
-    second_map = convolve(activated, kernels[1])
-    two_sum, two_square = moments(second_map, live_rows)
-    two_sum, two_square = lax.psum((two_sum, two_square), ("dp", "rep"))
+    second_map = convolve(activated, kernel_two)
+    two_sum, two_square = all_sum(moments(second_map, live_rows))
     normed_two, scale_two, pre_two = norm_apply(
         second_map, two_sum, two_square, norm_count, norm_gain[1], norm_bias[1]
     )
-    joined = feats.astype(jnp.float32) + pre_two
+    joined = feats_pos.astype(jnp.float32) + pre_two
     block_out = jax.nn.silu(joined)
-    pooled = (jnp.sum(block_out, axis=(1, 2)) / (map_side * map_side)).astype(jnp.bfloat16)
+    pooled = (jnp.sum(block_out, axis=(0, 1)) / area).astype(jnp.bfloat16)
     logits = jnp.dot(pooled, head_lowered, preferred_element_type=jnp.float32) + head_bias
     task_hot = (task_ids[:, None] == jnp.arange(TASKS)[None, :]).astype(jnp.float32)
     label_hot = (labels[:, None] == jnp.arange(CLASSES)[None, :]).astype(jnp.float32)
@@ -204,18 +313,28 @@
     dpooled = jnp.einsum("tsk,ck->tsc", dlogits, head_lowered, preferred_element_type=jnp.float32)
     head_part = jnp.einsum("sc,tsk->tck", pooled, dlogits, preferred_element_type=jnp.float32)
     bias_part = jnp.sum(dlogits.astype(jnp.float32), axis=1)
-    upstream = (dpooled / (map_side * map_side))[:, :, None, None, :] * silu_slope(joined)[None]
+    upstream = (dpooled / area)[:, None, None, :, :] * silu_slope(joined)[None]
     hidden_two, gain_two, shift_two = norm_back(
         upstream, normed_two, scale_two, norm_gain[1], live_rows, norm_count
     )
-    conv_two = layer_grad(activated, hidden_two)
-    act_grad = convolve_back(hidden_two, kernels[1]) * silu_slope(pre_one)[None]
+    shards_two = layer_grad(activated, hidden_two, nrep, ndp)
+    act_grad = convolve_back(hidden_two, kernel_two) * silu_slope(pre_one)[None]
     hidden_one, gain_one, shift_one = norm_back(
         act_grad, normed_one, scale_one, norm_gain[0], live_rows, norm_count
     )
-    conv_one = layer_grad(feats, hidden_one)
-    stacked = jnp.stack([conv_one, conv_two])
-    head_sum, bias_sum, loss_sum = lax.psum((head_part, bias_part, loss_terms), ("dp", "rep"))
+    shards_one = layer_grad(feats_pos, hidden_one, nrep, ndp)
+    head_pack = jnp.concatenate(
+        [head_part.transpose(1, 0, 2).reshape(channels, -1)]
+        + [jnp.zeros((channels, -2 * TASKS * CLASSES % 128), jnp.float32)],
+        axis=1,
+    )
+    tail = jnp.concatenate([bias_part.reshape(-1), loss_terms])
+    tail = jnp.pad(tail, (0, head_pack.shape[1] * 8 - tail.shape[0])).reshape(8, -1)
+    head_pack = all_sum(jnp.concatenate([head_pack, tail], axis=0))
+    tail = head_pack[channels:].reshape(-1)
+    head_sum = head_pack[:channels, : 2 * TASKS * CLASSES].reshape(channels, 2, -1).transpose(1, 0, 2)
+    bias_sum = tail[: 2 * TASKS * CLASSES].reshape(2, -1)
+    loss_sum = tail[2 * TASKS * CLASSES : 2 * TASKS * CLASSES + 2]
     norm_both = jnp.stack(
         [jnp.stack([gain_one, gain_two], axis=1), jnp.stack([shift_one, shift_two], axis=1)], axis=1
     )
@@ -229,27 +348,38 @@
         + jnp.sum(bias_sum[1] * bias_sum[1])
         + jnp.sum(norm_both[1] * norm_both[1])
     )
-    small_pair = jnp.stack([small_dot, small_square])
-    conv_sum = lax.psum(stacked, "dp")
+    parts = [[s.astype(jnp.float32) for s in shards] for shards in (shards_one, shards_two)]
+    flat = [s for shards in parts for s in shards]
     partial_value = jnp.stack(
         [
-            jnp.sum(conv_sum[:, :, 0] * conv_sum[:, :, 1]),
-            jnp.sum(conv_sum[:, :, 1] * conv_sum[:, :, 1]),
+            sum(jnp.sum(s[:, 0] * s[:, 1]) for s in flat),
+            sum(jnp.sum(s[:, 1] * s[:, 1]) for s in flat),
         ]
     )
-    agreement = lax.psum(partial_value, "rep") + small_pair
+    partial_value = jnp.broadcast_to(partial_value[:, None], (2, 128))
+    agreement = all_sum(partial_value)[:, 0] + jnp.stack([small_dot, small_square])
     project_coef = jnp.minimum(agreement[0], 0.0) / agreement[1]
-    conv_grad = conv_sum[:, :, 0] - project_coef * conv_sum[:, :, 1]
+    layers = []
+    for shards in parts:
+        gathered = []
+        for order, s in zip(orders(nrep, ndp), shards):
+            projected = (s[:, 0] - project_coef * s[:, 1]).astype(jnp.bfloat16)
+            whole = gather_dp(projected, order, ndp)
+            whole = whole.reshape((ndp,) + projected.shape).transpose(1, 0, 2, 3)
+            gathered.append(whole.reshape(-1, projected.shape[-1]))
+        layers.append(jnp.concatenate(gathered, axis=0))
+    conv_grad = jnp.stack(layers).astype(jnp.float32)
     conv_square = conv_grad * conv_grad + eps_one
     conv_cols_new = decay_rate * conv_cols + (1.0 - decay_rate) * jnp.mean(conv_square, axis=1)
     row_part = jnp.sum(conv_square, axis=2)
     over_cols = jnp.sum(conv_grad * conv_grad / conv_cols_new[:, None, :], axis=2)
     weight_part = jnp.sum(conv_master * conv_master, axis=(1, 2))
-    row_total, over_total, weight_total = (
-        lax.psum(row_part.astype(jnp.bfloat16), "rep").astype(jnp.float32),
-        lax.psum(over_cols.astype(jnp.bfloat16), "rep").astype(jnp.float32),
-        lax.psum(weight_part.astype(jnp.bfloat16), "rep").astype(jnp.float32),
-    )
+    weight_part = jnp.broadcast_to(weight_part[:, None], (2, 128))
+    row_pack = axis_sum(jnp.concatenate([row_part, over_cols, weight_part], axis=1), "rep")
+    count = row_part.shape[1]
+    row_total = row_pack[:, :count]
+    over_total = row_pack[:, count : 2 * count]
+    weight_total = row_pack[:, 2 * count]
     conv_rows_new = decay_rate * conv_rows + (1.0 - decay_rate) * row_total / channels
     row_mean = jnp.mean(conv_rows_new, axis=1)
     entries = conv_grad.shape[1] * channels
@@ -296,8 +426,14 @@
 
 
 def solution(mesh):
+    nrep = mesh.shape["rep"]
+    ndp = mesh.shape["dp"]
+
+    def run(*args):
+        return local(nrep, ndp, *args)
+
     return jax.shard_map(
-        local,
+        run,
         mesh=mesh,
         in_specs=(
             P(("dp", "rep"), None, None, None),

time: 1110 us -> 746 us (0.67)
  waiting for transfers between devices: 535 us -> 148 us
  blocking collectives: 188 us -> 0 us
  starting transfers between devices: 0.61 us -> 115 us
  local copies, waits for them, and re-layouts: 101 us -> 175 us
  other arithmetic: 76.4 us -> 118 us
  matrix products: 174 us -> 158 us
    psum x2 -> x0, waiting for transfers between devices: 404 us -> none  [the longest x1 298 us: local(): conv_sum = lax.psum(stacked, 'dp')]
    psum x6 -> x0, blocking collectives: 188 us -> none  [the longest x1 48.8 us: norm_back(): bias_grad, gain_grad = lax.psum((local_bias, local_gain), ('dp', 'rep'))]
    ppermute x0 -> x97, waiting for transfers between devices: none -> 148 us  [swap(): return lax.ppermute(x, axis, [(i, i ^ bit) for i in range(n)])]
    ppermute x0 -> x97, starting transfers between devices: none -> 115 us  [swap(): return lax.ppermute(x, axis, [(i, i ^ bit) for i in range(n)])]
    unnamed x121 -> x245, local copies, waits for them, and re-layouts: 98.9 us -> 6.95 us
    slice x0 -> x51, local copies, waits for them, and re-layouts: none -> 80.1 us  [the longest x47 77.3 us: convolve(): kernel[tap_index * channels:(tap_index + 1) * channels]]
    unnamed x7 -> x0, waiting for transfers between devices: 65.5 us -> none
    all_gather x1 -> x0, waiting for transfers between devices: 65.3 us -> none  [local(): lax.all_gather(conv_master.astype(jnp.bfloat16), 'rep', axis=2, tiled=True)]
  transfers between devices with their start and end apart: 5 -> 97, of which waited for: 4 -> 34; matrix products, arithmetic and copies ran while one was open for 16% -> 53% of each run, Pallas kernels for 0% -> 0%
where the time goes in v1:
time: 746 us; the launch traced here: 734 us
  local copies, waits for them, and re-layouts  175 us (23%)
  matrix products  158 us (21%)
  waiting for transfers between devices  148 us (20%)
  other arithmetic  118 us (16%)
  starting transfers between devices  115 us (15%)
  between operations  20.6 us (3%)
    ppermute x97, waiting for transfers between devices, swap(): return lax.ppermute(x, axis, [(i, i ^ bit) for i in range(n)])  148 us
    ppermute x97, starting transfers between devices, swap(): return lax.ppermute(x, axis, [(i, i ^ bit) for i in range(n)])  115 us
    slice x47, local copies, waits for them, and re-layouts, convolve(): kernel[tap_index * channels:(tap_index + 1) * channels]  77.3 us
    dot_general x9, matrix products, convolve_back(): jnp.einsum('tpqsd,cd->tpqsc', window, kernel[tap_index * channels:(tap_in...  56.9 us
    dot_general x18, matrix products, convolve(): jnp.einsum('pqsc,cd->pqsd', window, kernel[tap_index * channels:(tap_inde...  51.5 us
    dot_general x18, matrix products, layer_grad(): jnp.einsum('pqsc,tpqsd->tcd', window, grad_map, preferred_element_type=jn...  49.1 us
    dynamic_slice x11, local copies, waits for them, and re-layouts, pick(): return lax.dynamic_index_in_dim(x, index, dim, keepdims=False)  26.6 us
    transpose x18, local copies, waits for them, and re-layouts, layer_grad(): jnp.einsum('pqsc,tpqsd->tcd', window, grad_map, preferred_element_type=jn...  24.4 us
  transfers between devices with their start and end apart: 97, of which 34 were waited for; matrix products, arithmetic and copies ran while one was open for 53% of the time, Pallas kernels for 0%

profile of v1, /device:TPU:0, one launch (start us, length us, event | category | flops | bytes accessed | tf_op | source)
XLA Modules:
  0.0 733.9 jit_solution(9059007116425327777)
XLA Ops:
  0.7 5.2 multiply_reduce_fusion.2
  9.0 26.1 %collective-permute-done.9 = bf16[1,4608,128]{2,1,0:T(8,128)(2,1)} collective-permute-done((bf16[1,4608,128]{2,1,0:T(8,128)(2,1)S(1)}, bf16[1,4608,128]{2,1,0:T(8,128)(2,1)}, u32[]{:S(2)}, u32[]{:S(2)}) %collective-permute-start.9) | collective-permute-done | bytes 1179680 | tf_op jit(solution)/shard_map/ppermute | solution.py:20
  39.3 25.4 %collective-permute-done = bf16[1,4608,128]{2,1,0:T(8,128)(2,1)S(1)} collective-permute-done((bf16[1,4608,128]{2,1,0:T(8,128)(2,1)S(1)}, bf16[1,4608,128]{2,1,0:T(8,128)(2,1)S(1)}, u32[]{:S(2)}, u32[]{:S(2)}) %collective-permute-start) | collective-permute-done | bytes 1179680 | tf_op jit(solution)/shard_map/ppermute | solution.py:20
  97.9 4.3 fusion.156
  105.5 4.3 fusion.158
  113.1 4.6 fusion.160
  134.6 4.5 fusion.164
  139.1 4.3 fusion.166
  143.4 6.0 multiply_reduce_fusion.4
  191.7 4.8 add_multiply_fusion.1
  208.0 4.6 multiply_reduce_fusion.3
  249.6 5.3 add_multiply_fusion.2
  280.3 4.1 fusion.3
  284.5 4.4 fusion.130
  288.9 4.5 fusion.132
  293.4 4.4 fusion.128
  297.8 4.5 fusion.126
  302.3 4.4 fusion.124
  306.7 4.4 fusion.122
  311.1 4.4 fusion.120
  315.6 4.6 fusion.118
  320.2 21.2 %fusion.228 = (f32[2,512]{1,0:T(2,128)S(1)}, f32[2,512]{1,0:T(2,128)S(1)}, f32[2,4,4,96,512]{4,3,2,1,0:T(8,128)}) fusion(f32[4,4,96,512]{3,2,1,0:T(8,128)S(1)} %copy-done.3, f32[4,4,96,512]{3,2,1,0:T(8,128)} %get-tuple-element.76, bf16[2,4,4,96,512]{4,3,2,1,0:T(8,128)(2,1)S(1)} %fusion.3, bf16[512,512,1,1,1]{1,0,2,3,4:T(8,128)(2,1)} %reshape.636, ...), kind=kOutput, calls=%fused_computation.529 | convolution fusion | flops 924841984 | bytes 66592768 | tf_op jit(solution)/shard_map/tpqsd,cd->tpqsc/dot_general | solution.py:131
  460.4 4.4 pad_maximum_fusion.2
  481.6 8.1 %constant_dynamic-slice_fusion.11 = (bf16[2,1,2,2,2,3,2,64,128]{8,1,0,7,4,3,2,6,5:T(2,128)(2,1)}, bf16[2,1,2,2,2,3,2,64,128]{8,1,0,7,4,3,2,6,5:T(2,128)(2,1)S(1)}) fusion(bf16[2,2,2,2,2,3,2,64,128]{8,1,0,7,4,3,2,6,5:T(2,128)(2,1)S(1)} %bitcast.1023, s32[]{:T(128)S(6)} %select_n.367, s32[]{:T(128)S(6)} %select_n.368), kind=kLoop, calls=%fused_computation.416 | loop fusion | bytes 6291464 | tf_op jit(solution)/shard_map/jit(dynamic_index_in_dim)/dynamic_slice | solution.py:55
  520.3 10.7 %collective-permute-done.22 = f32[520,256]{1,0:T(8,128)S(1)} collective-permute-done((f32[520,256]{1,0:T(8,128)S(1)}, f32[520,256]{1,0:T(8,128)S(1)}, u32[]{:S(2)}, u32[]{:S(2)}) %collective-permute-start.22) | collective-permute-done | bytes 532512 | tf_op jit(solution)/shard_map/ppermute | solution.py:20
  531.0 15.5 %collective-permute-done.23 = f32[520,256]{1,0:T(8,128)S(1)} collective-permute-done((f32[520,256]{1,0:T(8,128)S(1)}, f32[520,256]{1,0:T(8,128)S(1)}, u32[]{:S(2)}, u32[]{:S(2)}) %collective-permute-start.23) | collective-permute-done | bytes 532512 | tf_op jit(solution)/shard_map/ppermute | solution.py:20
  555.4 9.6 %collective-permute-start.65 = (bf16[2,2,2,3,2,64,128]{6,5,3,4,0,2,1:T(8,128)(2,1)}, bf16[2,2,2,3,2,64,128]{6,5,3,4,0,2,1:T(8,128)(2,1)S(1)}, u32[]{:S(2)}, u32[]{:S(2)}) collective-permute-start(bf16[2,2,2,3,2,64,128]{6,5,3,4,0,2,1:T(8,128)(2,1)} %dynamic-slice_bitcast_fusion), channel_id=1, source_target_pairs={{0,8},{4,12},{8,0},{12,4},{16,24},{20,28},{24,16},{28,20},{1,9},{5... | collective-permute-start | bytes 2359304 | tf_op jit(solution)/shard_map/ppermute | solution.py:20
  578.5 5.1 collective-permute-done.65
  588.2 7.5 %collective-permute-start.66 = (bf16[2,2,3,2,64,128]{5,4,2,3,0,1:T(8,128)(2,1)S(1)}, bf16[2,2,3,2,64,128]{5,4,2,3,0,1:T(8,128)(2,1)S(1)}, u32[]{:S(2)}, u32[]{:S(2)}) collective-permute-start(bf16[2,2,3,2,64,128]{5,4,2,3,0,1:T(8,128)(2,1)S(1)} %dynamic-slice_bitcast_fusion.6), channel_id=1, source_target_pairs={{0,16},{4,20},{8,24},{12,28},{16,0},{20,4},{24,8},{28,12},{1,17},{... | collective-permute-start | bytes 1179656 | tf_op jit(solution)/shard_map/ppermute | solution.py:20
  597.6 8.3 %collective-permute-done.50 = bf16[2,2,2,3,2,64,128]{6,5,3,4,0,2,1:T(8,128)(2,1)S(1)} collective-permute-done((bf16[2,2,2,3,2,64,128]{6,5,3,4,0,2,1:T(8,128)(2,1)S(1)}, bf16[2,2,2,3,2,64,128]{6,5,3,4,0,2,1:T(8,128)(2,1)S(1)}, u32[]{:S(2)}, u32[]{:S(2)}) %collective-permute-start.50) | collective-permute-done | bytes 786464 | tf_op jit(solution)/shard_map/ppermute | solution.py:20
  609.7 9.4 %collective-permute-done.66 = bf16[2,2,3,2,64,128]{5,4,2,3,0,1:T(8,128)(2,1)S(1)} collective-permute-done((bf16[2,2,3,2,64,128]{5,4,2,3,0,1:T(8,128)(2,1)S(1)}, bf16[2,2,3,2,64,128]{5,4,2,3,0,1:T(8,128)(2,1)S(1)}, u32[]{:S(2)}, u32[]{:S(2)}) %collective-permute-start.66) | collective-permute-done | bytes 393248 | tf_op jit(solution)/shard_map/ppermute | solution.py:20
  632.1 4.2 collective-permute-done.47
  (794 shorter events, 470.1 us)
Async XLA Ops:
  6.0 29.1 %collective-permute-start.9 = (bf16[1,4608,128]{2,1,0:T(8,128)(2,1)S(1)}, bf16[1,4608,128]{2,1,0:T(8,128)(2,1)}, u32[]{:S(2)}, u32[]{:S(2)}) collective-permute-start(bf16[1,4608,128]{2,1,0:T(8,128)(2,1)S(1)} %slice.494), channel_id=1, source_target_pairs={{0,2},{1,3},{2,0},{3,1},{4,6},{5,7},{6,4},{7,5},{8,10},{9,11},{10,... | collective-permute-start | bytes 3538952 | tf_op jit(solution)/shard_map/ppermute | solution.py:20
  37.6 27.2 %collective-permute-start = (bf16[1,4608,128]{2,1,0:T(8,128)(2,1)S(1)}, bf16[1,4608,128]{2,1,0:T(8,128)(2,1)S(1)}, u32[]{:S(2)}, u32[]{:S(2)}) collective-permute-start(bf16[1,4608,128]{2,1,0:T(8,128)(2,1)S(1)} %get-tuple-element.122), channel_id=1, source_target_pairs={{0,2},{1,3},{2,0},{3,1},{4,6},{5,7},{6,4},{7,5},{8,10},{9,11},{10,... | collective-permute-start | bytes 3538952 | tf_op jit(solution)/shard_map/ppermute | solution.py:20
  75.9 77.5 %collective-permute-start.10 = (bf16[2,4608,128]{2,1,0:T(8,128)(2,1)}, bf16[2,4608,128]{2,1,0:T(8,128)(2,1)}, u32[]{:S(2)}, u32[]{:S(2)}) collective-permute-start(bf16[2,4608,128]{2,1,0:T(8,128)(2,1)} %maximum_bitcast_fusion.6), channel_id=1, source_target_pairs={{0,1},{1,0},{2,3},{3,2},{4,5},{5,4},{6,7},{7,6},{8,9},{9,8},{10,11... | collective-permute-start | bytes 7077896 | tf_op jit(solution)/shard_map/ppermute | solution.py:20
  159.7 30.1 %collective-permute-start.6 = (f32[1152]{0:T(1024)S(1)}, f32[1152]{0:T(1024)S(1)}, u32[]{:S(2)}, u32[]{:S(2)}) collective-permute-start(f32[1152]{0:T(1024)S(1)} %add.593), channel_id=1, source_target_pairs={{0,8},{4,12},{8,0},{12,4},{16,24},{20,28},{24,16},{28,20},{1,9},{5... | collective-permute-start | bytes 13832 | tf_op jit(solution)/shard_map/ppermute | solution.py:20
  161.3 28.5 %collective-permute-start.7 = (f32[1152]{0:T(1024)S(1)}, f32[1152]{0:T(1024)S(1)}, u32[]{:S(2)}, u32[]{:S(2)}) collective-permute-start(f32[1152]{0:T(1024)S(1)} %add.593), channel_id=1, source_target_pairs={{0,16},{4,20},{8,24},{12,28},{16,0},{20,4},{24,8},{28,12},{1,17},{... | collective-permute-start | bytes 13832 | tf_op jit(solution)/shard_map/ppermute | solution.py:20
  163.9 25.9 %collective-permute-start.8 = (f32[1152]{0:T(1024)S(1)}, f32[1152]{0:T(1024)S(1)}, u32[]{:S(2)}, u32[]{:S(2)}) collective-permute-start(f32[1152]{0:T(1024)S(1)} %add.593), channel_id=1, source_target_pairs={{0,24},{4,28},{8,16},{12,20},{16,8},{20,12},{24,0},{28,4},{1,25},{... | collective-permute-start | bytes 13832 | tf_op jit(solution)/shard_map/ppermute | solution.py:20
  217.2 22.1 %collective-permute-start.14 = (f32[2,512]{1,0:T(2,128)S(1)}, f32[2,512]{1,0:T(2,128)S(1)}, u32[]{:S(2)}, u32[]{:S(2)}) collective-permute-start(f32[2,512]{1,0:T(2,128)S(1)} %add_add_fusion.13), channel_id=1, source_target_pairs={{0,4},{4,0},{8,12},{12,8},{16,20},{20,16},{24,28},{28,24},{1,5},{5... | collective-permute-start | bytes 12296 | tf_op jit(solution)/shard_map/ppermute | solution.py:20
  278.6 211.1 %collective-permute-start.18 = (f32[520,256]{1,0:T(8,128)}, f32[520,256]{1,0:T(8,128)}, u32[]{:S(2)}, u32[]{:S(2)}) collective-permute-start(f32[520,256]{1,0:T(8,128)} %select_maximum_fusion), channel_id=1, source_target_pairs={{0,1},{1,0},{2,3},{3,2},{4,5},{5,4},{6,7},{7,6},{8,9},{9,8},{10,11... | collective-permute-start | bytes 1597448 | tf_op jit(solution)/shard_map/ppermute | solution.py:20
  278.6 211.5 %collective-permute-start.19 = (f32[520,256]{1,0:T(8,128)}, f32[520,256]{1,0:T(8,128)}, u32[]{:S(2)}, u32[]{:S(2)}) collective-permute-start(f32[520,256]{1,0:T(8,128)} %select_maximum_fusion), channel_id=1, source_target_pairs={{0,2},{1,3},{2,0},{3,1},{4,6},{5,7},{6,4},{7,5},{8,10},{9,11},{10,... | collective-permute-start | bytes 1597448 | tf_op jit(solution)/shard_map/ppermute | solution.py:20
  341.4 60.0 %collective-permute-start.32 = (f32[2,2,512]{2,0,1:T(2,128)S(1)}, f32[2,2,512]{2,0,1:T(2,128)S(1)}, u32[]{:S(2)}, u32[]{:S(2)}) collective-permute-start(f32[2,2,512]{2,0,1:T(2,128)S(1)} %pad_maximum_fusion.24), channel_id=1, source_target_pairs={{0,1},{1,0},{2,3},{3,2},{4,5},{5,4},{6,7},{7,6},{8,9},{9,8},{10,11... | collective-permute-start | bytes 24584 | tf_op jit(solution)/shard_map/ppermute | solution.py:20
  341.7 59.8 %collective-permute-start.33 = (f32[2,2,512]{2,0,1:T(2,128)S(1)}, f32[2,2,512]{2,0,1:T(2,128)S(1)}, u32[]{:S(2)}, u32[]{:S(2)}) collective-permute-start(f32[2,2,512]{2,0,1:T(2,128)S(1)} %pad_maximum_fusion.24), channel_id=1, source_target_pairs={{0,2},{1,3},{2,0},{3,1},{4,6},{5,7},{6,4},{7,5},{8,10},{9,11},{10,... | collective-permute-start | bytes 24584 | tf_op jit(solution)/shard_map/ppermute | solution.py:20
  342.8 58.7 %collective-permute-start.34 = (f32[2,2,512]{2,0,1:T(2,128)S(1)}, f32[2,2,512]{2,0,1:T(2,128)S(1)}, u32[]{:S(2)}, u32[]{:S(2)}) collective-permute-start(f32[2,2,512]{2,0,1:T(2,128)S(1)} %pad_maximum_fusion.24), channel_id=1, source_target_pairs={{0,3},{1,2},{2,1},{3,0},{4,7},{5,6},{6,5},{7,4},{8,11},{9,10},{10,... | collective-permute-start | bytes 24584 | tf_op jit(solution)/shard_map/ppermute | solution.py:20
  417.4 72.9 %collective-permute-start.20 = (f32[520,256]{1,0:T(8,128)}, f32[520,256]{1,0:T(8,128)}, u32[]{:S(2)}, u32[]{:S(2)}) collective-permute-start(f32[520,256]{1,0:T(8,128)} %select_maximum_fusion), channel_id=1, source_target_pairs={{0,3},{1,2},{2,1},{3,0},{4,7},{5,6},{6,5},{7,4},{8,11},{9,10},{10,... | collective-permute-start | bytes 1597448 | tf_op jit(solution)/shard_map/ppermute | solution.py:20
  417.4 89.5 %collective-permute-start.54 = (bf16[2,2,2,2,3,2,64,128]{7,6,4,5,1,2,3,0:T(8,128)(2,1)}, bf16[2,2,2,2,3,2,64,128]{7,6,4,5,1,2,3,0:T(8,128)(2,1)}, u32[]{:S(2)}, u32[]{:S(2)}) collective-permute-start(bf16[2,2,2,2,3,2,64,128]{7,6,4,5,1,2,3,0:T(8,128)(2,1)} %bitcast.1016), channel_id=1, source_target_pairs={{0,1},{1,0},{2,3},{3,2},{4,5},{5,4},{6,7},{7,6},{8,9},{9,8},{10,11... | collective-permute-start | bytes 4718600 | tf_op jit(solution)/shard_map/ppermute | solution.py:20
  418.5 95.3 %collective-permute-start.59 = (bf16[2,2,2,2,3,2,64,128]{7,6,4,5,1,2,0,3:T(8,128)(2,1)}, bf16[2,2,2,2,3,2,64,128]{7,6,4,5,1,2,0,3:T(8,128)(2,1)}, u32[]{:S(2)}, u32[]{:S(2)}) collective-permute-start(bf16[2,2,2,2,3,2,64,128]{7,6,4,5,1,2,0,3:T(8,128)(2,1)} %bitcast.1015), channel_id=1, source_target_pairs={{0,1},{1,0},{2,3},{3,2},{4,5},{5,4},{6,7},{7,6},{8,9},{9,8},{10,11... | collective-permute-start | bytes 4718600 | tf_op jit(solution)/shard_map/ppermute | solution.py:20
  489.7 27.8 %collective-permute-start.64 = (bf16[2,2,2,2,3,2,64,128]{7,6,4,5,0,3,1,2:T(8,128)(2,1)}, bf16[2,2,2,2,3,2,64,128]{7,6,4,5,0,3,1,2:T(8,128)(2,1)S(1)}, u32[]{:S(2)}, u32[]{:S(2)}) collective-permute-start(bf16[2,2,2,2,3,2,64,128]{7,6,4,5,0,3,1,2:T(8,128)(2,1)} %bitcast.1045), channel_id=1, source_target_pairs={{0,1},{1,0},{2,3},{3,2},{4,5},{5,4},{6,7},{7,6},{8,9},{9,8},{10,11... | collective-permute-start | bytes 4718600 | tf_op jit(solution)/shard_map/ppermute | solution.py:20
  490.1 65.2 %collective-permute-start.44 = (bf16[2,2,2,2,3,2,64,128]{7,6,4,5,1,2,0,3:T(8,128)(2,1)}, bf16[2,2,2,2,3,2,64,128]{7,6,4,5,1,2,0,3:T(8,128)(2,1)}, u32[]{:S(2)}, u32[]{:S(2)}) collective-permute-start(bf16[2,2,2,2,3,2,64,128]{7,6,4,5,1,2,0,3:T(8,128)(2,1)} %bitcast.1046), channel_id=1, source_target_pairs={{0,1},{1,0},{2,3},{3,2},{4,5},{5,4},{6,7},{7,6},{8,9},{9,8},{10,11... | collective-permute-start | bytes 4718600 | tf_op jit(solution)/shard_map/ppermute | solution.py:20
  506.6 24.4 %collective-permute-start.22 = (f32[520,256]{1,0:T(8,128)S(1)}, f32[520,256]{1,0:T(8,128)S(1)}, u32[]{:S(2)}, u32[]{:S(2)}) collective-permute-start(f32[520,256]{1,0:T(8,128)S(1)} %add.629), channel_id=1, source_target_pairs={{0,8},{4,12},{8,0},{12,4},{16,24},{20,28},{24,16},{28,20},{1,9},{5... | collective-permute-start | bytes 1597448 | tf_op jit(solution)/shard_map/ppermute | solution.py:20
  506.9 39.6 %collective-permute-start.23 = (f32[520,256]{1,0:T(8,128)S(1)}, f32[520,256]{1,0:T(8,128)S(1)}, u32[]{:S(2)}, u32[]{:S(2)}) collective-permute-start(f32[520,256]{1,0:T(8,128)S(1)} %add.629), channel_id=1, source_target_pairs={{0,16},{4,20},{8,24},{12,28},{16,0},{20,4},{24,8},{28,12},{1,17},{... | collective-permute-start | bytes 1597448 | tf_op jit(solution)/shard_map/ppermute | solution.py:20
  513.9 33.8 %collective-permute-start.24 = (f32[520,256]{1,0:T(8,128)S(1)}, f32[520,256]{1,0:T(8,128)S(1)}, u32[]{:S(2)}, u32[]{:S(2)}) collective-permute-start(f32[520,256]{1,0:T(8,128)S(1)} %add.629), channel_id=1, source_target_pairs={{0,24},{4,28},{8,16},{12,20},{16,8},{20,12},{24,0},{28,4},{1,25},{... | collective-permute-start | bytes 1597448 | tf_op jit(solution)/shard_map/ppermute | solution.py:20
  517.5 50.2 %collective-permute-start.39 = (bf16[2,2,2,2,3,2,64,128]{7,6,5,4,2,1,3,0:T(8,128)(2,1)}, bf16[2,2,2,2,3,2,64,128]{7,6,5,4,2,1,3,0:T(8,128)(2,1)}, u32[]{:S(2)}, u32[]{:S(2)}) collective-permute-start(bf16[2,2,2,2,3,2,64,128]{7,6,5,4,2,1,3,0:T(8,128)(2,1)} %bitcast.1019), channel_id=1, source_target_pairs={{0,1},{1,0},{2,3},{3,2},{4,5},{5,4},{6,7},{7,6},{8,9},{9,8},{10,11... | collective-permute-start | bytes 4718600 | tf_op jit(solution)/shard_map/ppermute | solution.py:20
  531.0 39.5 %collective-permute-start.49 = (bf16[2,2,2,2,3,2,64,128]{7,6,4,5,0,3,1,2:T(8,128)(2,1)}, bf16[2,2,2,2,3,2,64,128]{7,6,4,5,0,3,1,2:T(8,128)(2,1)}, u32[]{:S(2)}, u32[]{:S(2)}) collective-permute-start(bf16[2,2,2,2,3,2,64,128]{7,6,4,5,0,3,1,2:T(8,128)(2,1)} %bitcast.1017), channel_id=1, source_target_pairs={{0,1},{1,0},{2,3},{3,2},{4,5},{5,4},{6,7},{7,6},{8,9},{9,8},{10,11... | collective-permute-start | bytes 4718600 | tf_op jit(solution)/shard_map/ppermute | solution.py:20
  546.5 27.3 %collective-permute-start.55 = (bf16[2,2,2,3,2,64,128]{6,5,3,4,0,1,2:T(8,128)(2,1)}, bf16[2,2,2,3,2,64,128]{6,5,3,4,0,1,2:T(8,128)(2,1)}, u32[]{:S(2)}, u32[]{:S(2)}) collective-permute-start(bf16[2,2,2,3,2,64,128]{6,5,3,4,0,1,2:T(8,128)(2,1)} %dynamic-slice_bitcast_fusion.2), channel_id=1, source_target_pairs={{0,2},{1,3},{2,0},{3,1},{4,6},{5,7},{6,4},{7,5},{8,10},{9,11},{10,... | collective-permute-start | bytes 2359304 | tf_op jit(solution)/shard_map/ppermute | solution.py:20
  547.6 27.8 %collective-permute-start.60 = (bf16[2,2,2,3,2,64,128]{6,5,3,4,1,2,0:T(8,128)(2,1)}, bf16[2,2,2,3,2,64,128]{6,5,3,4,1,2,0:T(8,128)(2,1)}, u32[]{:S(2)}, u32[]{:S(2)}) collective-permute-start(bf16[2,2,2,3,2,64,128]{6,5,3,4,1,2,0:T(8,128)(2,1)} %dynamic-slice_bitcast_fusion.1), channel_id=1, source_target_pairs={{0,4},{4,0},{8,12},{12,8},{16,20},{20,16},{24,28},{28,24},{1,5},{5... | collective-permute-start | bytes 2359304 | tf_op jit(solution)/shard_map/ppermute | solution.py:20
  555.4 28.2 %collective-permute-start.65 = (bf16[2,2,2,3,2,64,128]{6,5,3,4,0,2,1:T(8,128)(2,1)}, bf16[2,2,2,3,2,64,128]{6,5,3,4,0,2,1:T(8,128)(2,1)S(1)}, u32[]{:S(2)}, u32[]{:S(2)}) collective-permute-start(bf16[2,2,2,3,2,64,128]{6,5,3,4,0,2,1:T(8,128)(2,1)} %dynamic-slice_bitcast_fusion), channel_id=1, source_target_pairs={{0,8},{4,12},{8,0},{12,4},{16,24},{20,28},{24,16},{28,20},{1,9},{5... | collective-permute-start | bytes 2359304 | tf_op jit(solution)/shard_map/ppermute | solution.py:20
  570.5 25.6 %collective-permute-start.40 = (bf16[2,2,2,3,2,64,128]{6,5,4,3,1,0,2:T(8,128)(2,1)S(1)}, bf16[2,2,2,3,2,64,128]{6,5,4,3,1,0,2:T(8,128)(2,1)S(1)}, u32[]{:S(2)}, u32[]{:S(2)}) collective-permute-start(bf16[2,2,2,3,2,64,128]{6,5,4,3,1,0,2:T(8,128)(2,1)S(1)} %dynamic-slice_bitcast_fusion.5), channel_id=1, source_target_pairs={{0,2},{1,3},{2,0},{3,1},{4,6},{5,7},{6,4},{7,5},{8,10},{9,11},{10,... | collective-permute-start | bytes 2359304 | tf_op jit(solution)/shard_map/ppermute | solution.py:20
  573.8 32.1 %collective-permute-start.50 = (bf16[2,2,2,3,2,64,128]{6,5,3,4,0,2,1:T(8,128)(2,1)S(1)}, bf16[2,2,2,3,2,64,128]{6,5,3,4,0,2,1:T(8,128)(2,1)S(1)}, u32[]{:S(2)}, u32[]{:S(2)}) collective-permute-start(bf16[2,2,2,3,2,64,128]{6,5,3,4,0,2,1:T(8,128)(2,1)S(1)} %dynamic-slice_bitcast_fusion.3), channel_id=1, source_target_pairs={{0,8},{4,12},{8,0},{12,4},{16,24},{20,28},{24,16},{28,20},{1,9},{5... | collective-permute-start | bytes 2359304 | tf_op jit(solution)/shard_map/ppermute | solution.py:20
  575.5 30.7 %collective-permute-start.56 = (bf16[2,2,3,2,64,128]{5,4,2,3,0,1:T(8,128)(2,1)S(1)}, bf16[2,2,3,2,64,128]{5,4,2,3,0,1:T(8,128)(2,1)S(1)}, u32[]{:S(2)}, u32[]{:S(2)}) collective-permute-start(bf16[2,2,3,2,64,128]{5,4,2,3,0,1:T(8,128)(2,1)S(1)} %dynamic-slice_bitcast_fusion.8), channel_id=1, source_target_pairs={{0,4},{4,0},{8,12},{12,8},{16,20},{20,16},{24,28},{28,24},{1,5},{5... | collective-permute-start | bytes 1179656 | tf_op jit(solution)/shard_map/ppermute | solution.py:20
  583.6 23.4 %collective-permute-start.61 = (bf16[2,2,3,2,64,128]{5,4,2,3,0,1:T(8,128)(2,1)S(1)}, bf16[2,2,3,2,64,128]{5,4,2,3,0,1:T(8,128)(2,1)S(1)}, u32[]{:S(2)}, u32[]{:S(2)}) collective-permute-start(bf16[2,2,3,2,64,128]{5,4,2,3,0,1:T(8,128)(2,1)S(1)} %dynamic-slice_bitcast_fusion.7), channel_id=1, source_target_pairs={{0,2},{1,3},{2,0},{3,1},{4,6},{5,7},{6,4},{7,5},{8,10},{9,11},{10,... | collective-permute-start | bytes 1179656 | tf_op jit(solution)/shard_map/ppermute | solution.py:20
  588.2 30.9 %collective-permute-start.66 = (bf16[2,2,3,2,64,128]{5,4,2,3,0,1:T(8,128)(2,1)S(1)}, bf16[2,2,3,2,64,128]{5,4,2,3,0,1:T(8,128)(2,1)S(1)}, u32[]{:S(2)}, u32[]{:S(2)}) collective-permute-start(bf16[2,2,3,2,64,128]{5,4,2,3,0,1:T(8,128)(2,1)S(1)} %dynamic-slice_bitcast_fusion.6), channel_id=1, source_target_pairs={{0,16},{4,20},{8,24},{12,28},{16,0},{20,4},{24,8},{28,12},{1,17},{... | collective-permute-start | bytes 1179656 | tf_op jit(solution)/shard_map/ppermute | solution.py:20
  596.0 23.2 %collective-permute-start.46 = (bf16[2,2,3,2,64,128]{5,4,2,3,0,1:T(8,128)(2,1)S(1)}, bf16[2,2,3,2,64,128]{5,4,2,3,0,1:T(8,128)(2,1)S(1)}, u32[]{:S(2)}, u32[]{:S(2)}) collective-permute-start(bf16[2,2,3,2,64,128]{5,4,2,3,0,1:T(8,128)(2,1)S(1)} %dynamic-slice_bitcast_fusion.10), channel_id=1, source_target_pairs={{0,2},{1,3},{2,0},{3,1},{4,6},{5,7},{6,4},{7,5},{8,10},{9,11},{10,... | collective-permute-start | bytes 1179656 | tf_op jit(solution)/shard_map/ppermute | solution.py:20
  606.2 20.6 %collective-permute-start.51 = (bf16[2,2,3,2,64,128]{5,4,2,3,0,1:T(8,128)(2,1)S(1)}, bf16[2,2,3,2,64,128]{5,4,2,3,0,1:T(8,128)(2,1)S(1)}, u32[]{:S(2)}, u32[]{:S(2)}) collective-permute-start(bf16[2,2,3,2,64,128]{5,4,2,3,0,1:T(8,128)(2,1)S(1)} %dynamic-slice_bitcast_fusion.9), channel_id=1, source_target_pairs={{0,16},{4,20},{8,24},{12,28},{16,0},{20,4},{24,8},{28,12},{1,17},{... | collective-permute-start | bytes 1179656 | tf_op jit(solution)/shard_map/ppermute | solution.py:20
  (184 other events, 2064.1 us)
